TPU v7x, 32 devices: a whole 2x2x4 slice. The times are simulated.
32 devices in a mesh: groups: 2 (over x), hist: 16 (over z, y, core).
Axes of the slice: x: 2, y: 2, z: 4, core: 2. Of those that a mesh axis runs over, the one named last changes fastest.
Arguments:
- queries: bfloat16 [256, 1536], P(('groups', 'hist')), parts along dimension 0, may hold values from -6 to 6
- keys_cache: bfloat16 [32768, 1536], P(('groups', 'hist')), parts along dimension 0, may hold values from -6 to 6
- values_cache: bfloat16 [32768, 1536], P(('groups', 'hist')), parts along dimension 0, may hold values from -6 to 6
- sel_blocks: int32 [64], P('groups'), parts along dimension 0, may hold values from 0 to 127, as said below
- hist_len: int32 [2], P('groups'), parts along dimension 0, may hold values from 8192 to 16384
- w_gate: bfloat16 [1536, 6144], P(None, 'hist'), may hold values from -0.15625 to 0.15625
- w_up: bfloat16 [1536, 6144], P(None, 'hist'), may hold values from -0.15625 to 0.15625
- w_down: bfloat16 [6144, 1536], P('hist'), may hold values from -0.078125 to 0.078125
Outputs:
- scored: bfloat16 [256, 1536], P(('groups', 'hist')), parts along dimension 0
There are 2 independent parts, one for each index of `groups`. A program takes and returns all parts, laid end to end along the dimension named above; an argument that names none is the same for every part. Nothing has to cross between parts.
Inputs may be any that keep to these rules, and one draw needn't show every extreme that they name: `sel_blocks`: ascending and distinct block numbers; block b holds keys b * 128 to (b + 1) * 128 - 1; of every aligned run of 8 blocks at most 4 are selected, and some run has exactly 4.
All inputs are finite; a program needn't handle non-finite values.
Results may differ from a plain program's by a relative error of at most 0.0051.
Values may be sent and summed in bfloat16 or wider, within the bound.
A program may use at most 128 MiB of HBM per device.

v0:
```python
import math

import jax
import jax.numpy as jnp
from jax import lax
from jax.sharding import PartitionSpec as P

HDIM = 128
BLOCK = 128


def rms_norm(values):
    return values * lax.rsqrt(jnp.mean(values * values, axis=-1, keepdims=True) + 1e-06)


def on_device(queries, keys_cache, values_cache, sel_blocks, hist_len, w_gate, w_up, w_down):
    hist_dev, model_width = keys_cache.shape
    head_count = model_width // HDIM
    blocks_dev = hist_dev // BLOCK
    my_index = lax.axis_index("hist")
    first_block = my_index * blocks_dev
    valid_len = hist_len[0]
    all_queries = lax.all_gather(queries, "hist", axis=0, tiled=True)
    own_blocks = first_block + jnp.arange(blocks_dev, dtype=jnp.int32)
    chosen = jnp.any(sel_blocks[:, None] == own_blocks[None, :], axis=0)
    positions = own_blocks[:, None] * BLOCK + jnp.arange(BLOCK, dtype=jnp.int32)[None, :]
    key_live = (chosen[:, None] & (positions < valid_len)).reshape(-1)
    live_weight = key_live.astype(jnp.float32)
    key_heads = keys_cache.reshape(-1, head_count, HDIM)
    value_heads = values_cache.reshape(-1, head_count, HDIM)
    total_rows = all_queries.shape[0]
    block_rows = min(512, total_rows)
    inv_scale = 1.0 / math.sqrt(HDIM)

    def attend(query_block):
        query_heads = query_block.reshape(block_rows, head_count, HDIM)
        scores = (
            jnp.einsum("qhd,khd->hqk", query_heads, key_heads, preferred_element_type=jnp.float32)
            * inv_scale
        )
        weights = (jax.nn.silu(scores) * live_weight[None, None, :]).astype(jnp.bfloat16)
        attended = jnp.einsum(
            "hqk,khd->qhd", weights, value_heads, preferred_element_type=jnp.float32
        )
        return attended.reshape(block_rows, model_width)

    partial_value = lax.map(
        attend, all_queries.reshape(total_rows // block_rows, block_rows, model_width)
    )
    partial_value = partial_value.reshape(total_rows, model_width)
    attention = lax.psum_scatter(partial_value, "hist", scatter_dimension=0, tiled=True)
    stream = queries.astype(jnp.float32) + rms_norm(attention)
    normed = rms_norm(stream).astype(jnp.bfloat16)
    normed_all = lax.all_gather(normed, "hist", axis=0, tiled=True)
    gate_proj = jnp.dot(normed_all, w_gate, preferred_element_type=jnp.float32)
    up_proj = jnp.dot(normed_all, w_up, preferred_element_type=jnp.float32)
    activation = (jax.nn.silu(gate_proj) * up_proj).astype(jnp.bfloat16)
    ffn_out = lax.psum_scatter(
        jnp.dot(activation, w_down, preferred_element_type=jnp.float32),
        "hist",
        scatter_dimension=0,
        tiled=True,
    )
    return (stream + ffn_out).astype(jnp.bfloat16)


def solution(mesh):
    placed = (
        P(("groups", "hist"), None),
        P(("groups", "hist"), None),
        P(("groups", "hist"), None),
        P("groups"),
        P("groups"),
        P(None, "hist"),
        P(None, "hist"),
        P("hist", None),
    )
    return jax.shard_map(
        on_device,
        mesh=mesh,
        in_specs=placed,
        out_specs=P(("groups", "hist"), None),
        check_vma=False,
    )
```

profile of v0, /device:TPU:0, one launch (start us, length us, event | category | flops | bytes accessed | tf_op | source)
XLA Modules:
  0.0 191.9 jit_solution(17600822007273147206)
XLA Ops:
  6.5 0.0 copy-start
  6.5 0.0 reduce-scatter.3.cloned.1.call-start
  7.3 24.4 %all_gather.6 = bf16[128,1536]{1,0:T(8,128)(2,1)S(1)} all-gather(bf16[8,1536]{1,0:T(8,128)(2,1)} %param.8), channel_id=1, replica_groups=mesh['groups'=2,'hist'=16] {'hist'}, dimensions={0}, use_global_device_ids=true | all-gather | bytes 417792 | tf_op jit(solution)/shard_map/all_gather | solution.py:23
  31.7 0.2 copy.24
  31.9 4.7 %copy.25 = bf16[1024,1536]{0,1:T(8,128)(2,1)} copy(bf16[1024,1536]{1,0:T(8,128)(2,1)} %param.9) | data formatting | bytes 6291456 | tf_op args[1]
  36.6 0.0 copy-start.5
  36.6 4.7 %copy.28 = bf16[1024,1536]{0,1:T(8,128)(2,1)} copy(bf16[1024,1536]{1,0:T(8,128)(2,1)} %param.10) | data formatting | bytes 6291456 | tf_op args[2]
  41.3 0.0 copy-done.5
  41.3 0.2 compare_reduce_fusion
  41.5 0.1 convert_bitcast_fusion
  41.6 0.0 copy-start.3
  41.6 6.4 %fusion = f32[12,128,128]{1,2,0:T(8,128)S(1)} fusion(bf16[1024,12,128]{0,2,1:T(8,128)(2,1)} %bitcast.19, f32[1024]{0:T(1024)S(1)} %convert_bitcast_fusion, bf16[128,12,128]{0,2,1:T(8,128)(2,1)S(1)} %bitcast.21, bf16[1024,12,128]{0,2,1:T(8,128)(2,1)} %bitcast.18), kind=kOutput, calls=%fused_computation.1 | convolution fusion | flops 816316416 | bytes 7475200 | tf_op jit(solution)/shard_map/while/body/eval_jaxpr/hqk,khd->qhd/dot_general | solution.py:42
  47.9 0.0 copy-start.1
  47.9 1.1 copy.29
  49.1 0.0 reduce-scatter.3.cloned.1.call-update
  49.1 0.0 reduce-scatter.5.cloned.1.call-start
  49.1 53.9 %reduce-scatter.3.cloned.1.call-done = f32[8,1536]{1,0:T(8,128)} async-done(((f32[128,1536]{1,0:T(8,128)}), f32[8,1536]{1,0:T(8,128)}) %reduce-scatter.3.cloned.1.call-update) | async-done | bytes 49168 | tf_op jit(solution)/shard_map/reduce_scatter | solution.py:51
  103.1 0.9 multiply_reduce_fusion.1
  104.0 0.0 copy-done.3
  104.0 1.0 multiply_reduce_fusion
  105.0 0.9 multiply_convert_fusion.2
  105.9 20.4 %all_gather.7 = bf16[128,1536]{1,0:T(8,128)(2,1)S(1)} all-gather(bf16[8,1536]{1,0:T(8,128)(2,1)S(1)} %multiply_convert_fusion.2), channel_id=1, replica_groups=mesh['groups'=2,'hist'=16] {'hist'}, dimensions={0}, use_global_device_ids=true | all-gather | bytes 417792 | tf_op jit(solution)/shard_map/all_gather | solution.py:54
  126.3 0.0 copy-start.2
  126.3 0.0 copy-start.4
  126.3 1.6 fusion.15
  128.0 0.0 copy-done
  128.0 0.0 copy-done.1
  128.0 1.6 fusion.4
  129.6 0.0 reduce-scatter.5.cloned.1.call-update
  129.6 54.0 %reduce-scatter.5.cloned.1.call-done = f32[8,1536]{1,0:T(8,128)} async-done(((f32[128,1536]{1,0:T(8,128)}), f32[8,1536]{1,0:T(8,128)}) %reduce-scatter.5.cloned.1.call-update) | async-done | bytes 49168 | tf_op jit(solution)/shard_map/reduce_scatter | solution.py:58
  183.6 0.0 copy-done.2
  183.6 0.0 copy-done.4
  183.6 1.5 add_convert_fusion
  (4 shorter events, 0.0 us)
Async XLA Ops:
  6.5 121.4 %copy-start = (bf16[384,1536]{1,0:T(8,128)(2,1)S(1)}, bf16[384,1536]{1,0:T(8,128)(2,1)}, u32[]{:S(2)}) copy-start(bf16[384,1536]{1,0:T(8,128)(2,1)} %param.15) | copy-start | bytes 3538948
  6.5 96.5 %reduce-scatter.3.cloned.1.call-start = ((), (), s32[]{:S(2)}) async-start(), calls=%async_computation.2 | async-start | bytes 835584 | tf_op jit(solution)/shard_map/reduce_scatter | solution.py:51
  36.6 4.7 %copy-start.5 = (s32[32]{0:T(128)S(1)}, s32[32]{0:T(128)}, u32[]{:S(2)}) copy-start(s32[32]{0:T(128)} %param.11) | copy-start | bytes 388
  41.6 62.5 %copy-start.3 = (bf16[8,1536]{1,0:T(8,128)(2,1)S(1)}, bf16[8,1536]{1,0:T(8,128)(2,1)}, u32[]{:S(2)}) copy-start(bf16[8,1536]{1,0:T(8,128)(2,1)} %param.8) | copy-start | bytes 73732
  47.9 80.1 %copy-start.1 = (bf16[1536,384]{1,0:T(8,128)(2,1)S(1)}, bf16[1536,384]{1,0:T(8,128)(2,1)}, u32[]{:S(2)}) copy-start(bf16[1536,384]{1,0:T(8,128)(2,1)} %param.14) | copy-start | bytes 3538948
  49.1 134.5 %reduce-scatter.5.cloned.1.call-start = ((), (), s32[]{:S(2)}) async-start(), calls=%async_computation.3 | async-start | bytes 835584 | tf_op jit(solution)/shard_map/reduce_scatter | solution.py:58
  126.3 57.3 %copy-start.2 = (f32[8,1536]{1,0:T(8,128)S(1)}, f32[8,1536]{1,0:T(8,128)}, u32[]{:S(2)}) copy-start(f32[8,1536]{1,0:T(8,128)} %reduce-scatter.3.cloned.1.call-done) | copy-start | bytes 147460
  126.3 57.3 %copy-start.4 = (bf16[8,1536]{1,0:T(8,128)(2,1)S(1)}, bf16[8,1536]{1,0:T(8,128)(2,1)}, u32[]{:S(2)}) copy-start(bf16[8,1536]{1,0:T(8,128)(2,1)} %param.8) | copy-start | bytes 73732
Sparse Core Ops, SparseCore 0:
  49.2 53.8 reduce-scatter.2
  129.7 53.8 reduce-scatter.4
where the time goes:
time: 192 us
  waiting for transfers between devices  108 us (56%)
  blocking collectives  44.8 us (23%)
  between operations  14.2 us (7%)
  local copies, waits for them, and re-layouts  10.7 us (6%)
  matrix products  9.57 us (5%)
  other arithmetic  4.56 us (2%)
    reduce_scatter x1, waiting for transfers between devices, on_device(): lax.psum_scatter(jnp.dot(activation, w_down, preferred_element_type=jnp.f...  54 us
    reduce_scatter x1, waiting for transfers between devices, on_device(): lax.psum_scatter(partial_value, 'hist', scatter_dimension=0, tiled=True)  53.9 us
    all_gather x1, blocking collectives, on_device(): all_queries = lax.all_gather(queries, 'hist', axis=0, tiled=True)  24.4 us
    all_gather x1, blocking collectives, on_device(): normed_all = lax.all_gather(normed, 'hist', axis=0, tiled=True)  20.4 us
    unnamed x14, local copies, waits for them, and re-layouts  9.38 us
    dot_general x1, matrix products, attend(): jnp.einsum('hqk,khd->qhd', weights, value_heads, preferred_element_type=j...  6.36 us
  transfers between devices with their start and end apart: 2, of which 2 were waited for; matrix products, arithmetic and copies ran while one was open for 0% of the time, Pallas kernels for 0%

commit v1 on v0

v1 whole, which is shorter than its diff:
```python
import functools
import math

import jax
import jax.numpy as jnp
from jax import lax
from jax.experimental import pallas as pl
from jax.experimental.pallas import tpu as pltpu
from jax.sharding import PartitionSpec as P

HDIM = 128
BLOCK = 128
CORES = 2
MESH = pl.DeviceIdType.MESH
F32 = jnp.float32
BF16 = jnp.bfloat16


def loop(start, stop, body):
    if stop - start <= 8:
        for i in range(start, stop):
            body(i)
    else:
        lax.fori_loop(start, stop, lambda i, c: (body(i), c)[1], 0)


def silu_of_twice(z):
    return z + z * jnp.tanh(z)


def pack(rows):
    half = rows.shape[1] // 2
    return jnp.concatenate([rows[:, :half], rows[:, half:]], axis=0)


def unpack(rows):
    half = rows.shape[0] // 2
    return jnp.concatenate([rows[:half], rows[half:]], axis=1)


def rms_scale(packed):
    half, width = packed.shape[0] // 2, packed.shape[1] * 2
    squares = jnp.sum(packed * packed, axis=1, keepdims=True)
    both = lax.rsqrt((squares[:half] + squares[half:]) / width + 1e-06)
    return jnp.concatenate([both, both], axis=0)


def kernel(
    chips, sel_ref, len_ref, q_ref, k_hbm, v_hbm, wg_hbm, wu_hbm, wd_hbm, out_ref,
    qbuf, nbuf, keep_a, stage_a, cbuf_a, obuf_a, rbuf_a, keep_f, stage_f, cbuf_f, obuf_f, rbuf_f,
    k_all, v_all, k_sel, v_sel, wg, wu, wd,
    local_sem, q_send, q_recv, qf_send, qf_recv, n_send, n_recv, nf_send, nf_recv,
    a_send, a_recv, f_send, f_recv, c_send, c_recv,
):
    tokens, width = q_ref.shape
    half = width // 2
    pairs = half // HDIM
    slots = k_sel.shape[0]
    blocks_dev = k_all.shape[0]
    chunk = min(chips, 8)
    group = lax.axis_index("groups")
    me = lax.axis_index("hist")
    chip, core = me // CORES, me % CORES
    sibling = (group, chip * CORES + (1 - core))

    def peer(offset):
        return (group, lax.rem(chip + offset, chips) * CORES + core)

    locals_ = [
        pltpu.make_async_copy(src, dst, local_sem.at[i])
        for i, (src, dst) in enumerate(
            [(k_hbm, k_all), (v_hbm, v_all), (wg_hbm, wg), (wu_hbm, wu), (wd_hbm, wd)]
        )
    ]
    for copy in locals_:
        copy.start()

    barrier = pltpu.get_barrier_semaphore()
    pl.semaphore_signal(barrier, inc=1, device_id=sibling, device_id_type=MESH)
    loop(1, chips, lambda k: pl.semaphore_signal(barrier, inc=1, device_id=peer(k), device_id_type=MESH))

    q_packed = pack(q_ref[...].astype(F32))
    qbuf[0, 0] = q_packed.astype(BF16)
    pl.semaphore_wait(barrier, chips)

    class Gather:
        def __init__(self, buf, send, recv, fsend, frecv):
            self.buf, self.sems = buf, (send, recv, fsend, frecv)

        def out(self, k):
            send, recv, _, _ = self.sems
            return pltpu.make_async_remote_copy(
                self.buf.at[0, 0], self.buf.at[0, k], send.at[k], recv.at[k], peer(k), MESH
            )

        def forward(self, k):
            _, _, fsend, frecv = self.sems
            return pltpu.make_async_remote_copy(
                self.buf.at[0, k], self.buf.at[1, k], fsend.at[k], frecv.at[k], sibling, MESH
            )

        def start(self):
            loop(1, chips, lambda k: self.out(k).start())
            self.forward(0).start()

        def finish(self):
            def step(k):
                self.out(k).wait_recv()
                self.forward(k).start()

            loop(1, chips, step)
            loop(0, chips, lambda k: self.forward(k).wait_recv())

        def drain(self):
            loop(1, chips, lambda k: self.out(k).wait_send())
            loop(0, chips, lambda k: self.forward(k).wait_send())

    class Scatter:
        def __init__(self, index, keep, stage, cbuf, obuf, rbuf, send, recv):
            self.keep, self.stage, self.cbuf, self.obuf, self.rbuf = keep, stage, cbuf, obuf, rbuf
            self.index, self.send, self.recv = index, send, recv

        def across(self):
            return pltpu.make_async_remote_copy(
                self.stage, self.cbuf, c_send.at[self.index], c_recv.at[self.index], sibling, MESH
            )

        def out(self, k):
            return pltpu.make_async_remote_copy(
                self.obuf.at[k], self.rbuf.at[k], self.send.at[k], self.recv.at[k], peer(chips - k), MESH
            )

        def total(self):
            self.across().start()
            self.across().wait_recv()

            def step(k):
                self.obuf[k] = (self.keep[k] + self.cbuf[k].astype(F32)).astype(BF16)
                self.out(k).start()

            loop(1, chips, step)
            total = self.keep[0] + self.cbuf[0].astype(F32)
            if chips <= 8:
                for k in range(1, chips):
                    self.out(k).wait_recv()
                    total = total + self.rbuf[k].astype(F32)
                return total

            def add(k, total):
                self.out(k).wait_recv()
                return total + self.rbuf[k].astype(F32)

            return lax.fori_loop(1, chips, add, total)

        def drain(self):
            self.across().wait_send()
            loop(1, chips, lambda k: self.out(k).wait_send())

    queries = Gather(qbuf, q_send, q_recv, qf_send, qf_recv)
    attended = Scatter(0, keep_a, stage_a, cbuf_a, obuf_a, rbuf_a, a_send, a_recv)
    normals = Gather(nbuf, n_send, n_recv, nf_send, nf_recv)
    hidden = Scatter(1, keep_f, stage_f, cbuf_f, obuf_f, rbuf_f, f_send, f_recv)

    queries.start()

    first = me * blocks_dev

    def pick(i, state):
        count, chosen, used = state
        local = sel_ref[i] - first
        mine = jnp.logical_and(local >= 0, local < blocks_dev)
        hit = [jnp.logical_and(mine, count == s) for s in range(slots)]
        chosen = tuple(jnp.where(h, local, c) for h, c in zip(hit, chosen))
        return count + mine.astype(jnp.int32), chosen, used

    zero = jnp.int32(0)
    count, chosen, _ = lax.fori_loop(0, sel_ref.shape[0], pick, (zero, (zero,) * slots, zero))
    row = lax.broadcasted_iota(jnp.int32, (BLOCK, 1), 0)
    locals_[0].wait()
    for s in range(slots):
        k_sel[s] = k_all[chosen[s]]
    locals_[1].wait()
    for s in range(slots):
        limit = jnp.where(count > s, len_ref[0] - (first + chosen[s]) * BLOCK, 0)
        block = v_all[chosen[s]]
        v_sel[s] = jnp.where(row < limit, block.astype(F32), 0.0).astype(BF16)

    queries.finish()

    half_scale = 0.5 / math.sqrt(HDIM)

    def head(query, columns):
        keys = k_sel[:, :, columns].reshape(slots * BLOCK, HDIM)
        values = v_sel[:, :, columns].reshape(slots * BLOCK, HDIM)
        scores = lax.dot_general(query, keys, (((1,), (1,)), ((), ())), preferred_element_type=F32)
        weights = silu_of_twice(scores * half_scale).astype(BF16)
        return jnp.dot(weights, values, preferred_element_type=F32)

    def halves(block):
        w = block.shape[-1]
        block = block.astype(F32).reshape(2 * chunk, 2, tokens, w)
        return [block[:, i].reshape(2 * chunk * tokens, w).astype(BF16) for i in range(2)]

    def joined(left, right):
        w = left.shape[-1]
        parts = [x.reshape(2, chunk, tokens, w) for x in (left, right)]
        return jnp.concatenate(parts, axis=2)

    def attend(i):
        rows = pl.ds(i * chunk, chunk)
        for j in range(pairs):
            columns = pl.ds(j * HDIM, HDIM)
            left, right = halves(qbuf[:, rows, :, columns])
            both = joined(head(left, columns), head(right, pl.ds(half + j * HDIM, HDIM)))
            keep_a[rows, :, columns] = both[0]
            stage_a[rows, :, columns] = both[1].astype(BF16)

    loop(0, chips // chunk, attend)

    attention = attended.total()
    stream = q_packed + attention * rms_scale(attention)
    nbuf[0, 0] = (stream * rms_scale(stream)).astype(BF16)
    normals.start()
    for copy in locals_[2:]:
        copy.wait()
    normals.finish()

    step_columns = 256 if half % 256 == 0 else HDIM

    def feed(i):
        rows = pl.ds(i * chunk, chunk)
        left, right = halves(nbuf[:, rows])

        def project(w):
            top = jnp.dot(left, w[:half], preferred_element_type=F32)
            return top + jnp.dot(right, w[half:], preferred_element_type=F32)

        activation = (silu_of_twice(0.5 * project(wg)) * project(wu)).astype(BF16)
        for j in range(half // step_columns):
            columns = pl.ds(j * step_columns, step_columns)
            both = joined(
                jnp.dot(activation, wd[:, columns], preferred_element_type=F32),
                jnp.dot(activation, wd[:, pl.ds(half + j * step_columns, step_columns)], preferred_element_type=F32),
            )
            keep_f[rows, :, columns] = both[0]
            stage_f[rows, :, columns] = both[1].astype(BF16)

    loop(0, chips // chunk, feed)

    out_ref[...] = unpack(stream + hidden.total()).astype(out_ref.dtype)

    queries.drain()
    attended.drain()
    normals.drain()
    hidden.drain()


def on_device(hist, queries, keys_cache, values_cache, sel_blocks, hist_len, w_gate, w_up, w_down):
    chips = hist // CORES
    tokens, width = queries.shape
    blocks_dev = keys_cache.shape[0] // BLOCK
    slots = max(1, blocks_dev // 2)
    hidden = w_gate.shape[1]
    blocked = (blocks_dev, BLOCK, width)
    packed = (2 * tokens, width // 2)
    exchange = [
        pltpu.VMEM((chips,) + packed, F32),
        pltpu.VMEM((chips,) + packed, BF16),
        pltpu.VMEM((chips,) + packed, BF16),
        pltpu.VMEM((chips,) + packed, BF16),
        pltpu.VMEM((chips,) + packed, BF16),
    ]
    smem = pl.BlockSpec(memory_space=pltpu.SMEM)
    vmem = pl.BlockSpec(memory_space=pltpu.VMEM)
    anywhere = pl.BlockSpec(memory_space=pl.ANY)
    return pl.pallas_call(
        functools.partial(kernel, chips),
        out_shape=jax.ShapeDtypeStruct((tokens, width), BF16),
        in_specs=[smem, smem, vmem] + [anywhere] * 5,
        out_specs=vmem,
        scratch_shapes=[
            pltpu.VMEM((2, chips) + packed, BF16),
            pltpu.VMEM((2, chips) + packed, BF16),
            *exchange,
            *exchange,
            pltpu.VMEM(blocked, BF16),
            pltpu.VMEM(blocked, BF16),
            pltpu.VMEM((slots, BLOCK, width), BF16),
            pltpu.VMEM((slots, BLOCK, width), BF16),
            pltpu.VMEM((width, hidden), BF16),
            pltpu.VMEM((width, hidden), BF16),
            pltpu.VMEM((hidden, width), BF16),
            pltpu.SemaphoreType.DMA((5,)),
            *[pltpu.SemaphoreType.DMA((chips,))] * 12,
            pltpu.SemaphoreType.DMA((2,)),
            pltpu.SemaphoreType.DMA((2,)),
        ],
        compiler_params=pltpu.CompilerParams(
            collective_id=0, has_side_effects=True, vmem_limit_bytes=56 * 1024 * 1024
        ),
    )(
        sel_blocks, hist_len, queries, keys_cache.reshape(blocked), values_cache.reshape(blocked),
        w_gate, w_up, w_down,
    )


def solution(mesh):
    placed = (
        P(("groups", "hist"), None),
        P(("groups", "hist"), None),
        P(("groups", "hist"), None),
        P("groups"),
        P("groups"),
        P(None, "hist"),
        P(None, "hist"),
        P("hist", None),
    )
    return jax.shard_map(
        functools.partial(on_device, mesh.shape["hist"]),
        mesh=mesh,
        in_specs=placed,
        out_specs=P(("groups", "hist"), None),
        check_vma=False,
    )
```

time: 192 us -> 42 us (0.22)
  waiting for transfers between devices: 108 us -> 0 us
  blocking collectives: 44.8 us -> 0 us
  Pallas kernels: 0 us -> 39.8 us
  between operations: 14.2 us -> 0.66 us
  matrix products: 9.57 us -> 0 us
  local copies, waits for them, and re-layouts: 10.7 us -> 1.35 us
  other arithmetic: 4.56 us -> 0 us
    reduce_scatter x2 -> x0, waiting for transfers between devices: 108 us -> none  [the longest x1 54 us: on_device(): lax.psum_scatter(jnp.dot(activation, w_down, preferred_element_type=jnp.f...]
    all_gather x2 -> x0, blocking collectives: 44.8 us -> none  [the longest x1 24.4 us: on_device(): all_queries = lax.all_gather(queries, 'hist', axis=0, tiled=True)]
    pallas_call x0 -> x1, Pallas kernels: none -> 39.8 us  [on_device(): pl.pallas_call(functools.partial(kernel, chips), out_shape=jax.ShapeDtype...]
    dot_general x3 -> x0, matrix products: 9.57 us -> none  [the longest x1 6.36 us: attend(): jnp.einsum('hqk,khd->qhd', weights, value_heads, preferred_element_type=j...]
    unnamed x14 -> x1, local copies, waits for them, and re-layouts: 9.38 us -> 1.35 us
    convert_element_type x3 -> x0, other arithmetic: 2.44 us -> none  [the longest x1 1.48 us: on_device(): return (stream + ffn_out).astype(jnp.bfloat16)]
  transfers between devices with their start and end apart: 2 -> 0, of which waited for: 2 -> 0; matrix products, arithmetic and copies ran while one was open for 0% -> 0% of each run, Pallas kernels for 0% -> 0%
where the time goes in v1:
time: 42 us; the launch traced here: 41.8 us
  Pallas kernels  39.8 us (95%)
  local copies, waits for them, and re-layouts  1.35 us (3%)
  between operations  0.66 us (2%)
    pallas_call x1, Pallas kernels, on_device(): pl.pallas_call(functools.partial(kernel, chips), out_shape=jax.ShapeDtype...  39.8 us
    unnamed x1, local copies, waits for them, and re-layouts  1.35 us

profile of v1, /device:TPU:0, one launch (start us, length us, event | category | flops | bytes accessed | tf_op | source)
XLA Modules:
  0.0 41.8 jit_solution(13194234694074060790)
XLA Ops:
  0.7 39.8 %shard_map.82 = bf16[8,1536]{1,0:T(8,128)(2,1)} custom-call(s32[32]{0:T(128)} %sel_ref.1, s32[1]{0:T(128)S(6)} %copy.10.len_ref, bf16[8,1536]{1,0:T(8,128)(2,1)} %q_ref.1, bf16[8,128,1536]{2,1,0:T(8,128)(2,1)} %bitcast.2, bf16[8,128,1536]{2,1,0:T(8,128)(2,1)} %bitcast.3, bf16[1536,384]{1,0:T(8,128)(2,1)} %wg_hbm.1, bf16[1536,384]{1,0:T(8,128)(2,1)} %wu_hbm.1, ...), custom_call_target="tpu_custom_call" | custom-call | tf_op jit(solution)/shard_map/pallas_call | solution.py:276
  40.4 1.3 %copy.11 = bf16[8,1536]{1,0:T(8,128)(2,1)} copy(bf16[8,1536]{1,0:T(8,128)(2,1)} %shard_map.82) | data formatting | bytes 49152

commit v2 on v1

v2 whole, which is shorter than its diff:
```python
import functools
import math

import jax
import jax.numpy as jnp
from jax import lax
from jax.experimental import pallas as pl
from jax.experimental.pallas import tpu as pltpu
from jax.sharding import PartitionSpec as P

HDIM = 128
BLOCK = 128
CORES = 2
COLUMN_GROUPS = 3
MESH = pl.DeviceIdType.MESH
F32 = jnp.float32
BF16 = jnp.bfloat16


def loop(start, stop, body):
    if stop - start <= 8:
        for i in range(start, stop):
            body(i)
    else:
        lax.fori_loop(start, stop, lambda i, c: (body(i), c)[1], 0)


def silu_of_twice(z):
    return z + z * jnp.tanh(z)


def pack(rows):
    half = rows.shape[1] // 2
    return jnp.concatenate([rows[:, :half], rows[:, half:]], axis=0)


def unpack(rows):
    half = rows.shape[0] // 2
    return jnp.concatenate([rows[:half], rows[half:]], axis=1)


def rms_scale(packed):
    half, width = packed.shape[0] // 2, packed.shape[1] * 2
    squares = jnp.sum(packed * packed, axis=1, keepdims=True)
    both = lax.rsqrt((squares[:half] + squares[half:]) / width + 1e-06)
    return jnp.concatenate([both, both], axis=0)


def kernel(
    chips, sel_ref, len_ref, q_ref, k_hbm, v_hbm, wg_hbm, wu_hbm, wd_hbm, out_ref,
    qbuf, nbuf, keep_a, obuf_a, rbuf_a, keep_f, obuf_f, rbuf_f,
    k_all, v_all, k_sel, v_sel, wg, wu, wd,
    local_sem, pair_send, pair_recv, q_send, q_recv, n_send, n_recv, a_send, a_recv, f_send, f_recv,
):
    tokens, width = q_ref.shape
    half = width // 2
    groups, span = keep_a.shape[0], keep_a.shape[2]
    slots = k_sel.shape[1]
    blocks_dev = k_all.shape[0]
    chunk = min(chips, 8)
    group = lax.axis_index("groups")
    me = lax.axis_index("hist")
    chip, core = me // CORES, me % CORES
    sibling = (group, chip * CORES + (1 - core))
    paired = chips & (chips - 1) == 0

    def peer(k, back=False):
        if paired:
            other = jnp.bitwise_xor(chip, k)
        else:
            other = lax.rem(chip + (chips - k if back else k), chips)
        return (group, other * CORES + core)

    def peers(body):
        loop(1, chips, lambda i: body(chips - i))

    locals_ = [
        pltpu.make_async_copy(src, dst, local_sem.at[i])
        for i, (src, dst) in enumerate(
            [(k_hbm, k_all), (v_hbm, v_all), (wg_hbm, wg.at[0]), (wu_hbm, wu.at[0]), (wd_hbm, wd.at[0])]
        )
    ]
    for copy in locals_:
        copy.start()

    barrier = pltpu.get_barrier_semaphore()
    pl.semaphore_signal(barrier, inc=1, device_id=sibling, device_id_type=MESH)
    peers(lambda k: pl.semaphore_signal(barrier, inc=1, device_id=peer(k), device_id_type=MESH))

    q_packed = pack(q_ref[...].astype(F32))
    qbuf[0] = q_packed.astype(BF16)

    first = me * blocks_dev

    def pick(i, state):
        count, chosen = state
        local = sel_ref[i] - first
        mine = jnp.logical_and(local >= 0, local < blocks_dev)
        hit = [jnp.logical_and(mine, count == s) for s in range(slots)]
        return count + mine.astype(jnp.int32), tuple(jnp.where(h, local, c) for h, c in zip(hit, chosen))

    zero = jnp.int32(0)
    count, chosen = lax.fori_loop(0, sel_ref.shape[0], pick, (zero, (zero,) * slots))
    row = lax.broadcasted_iota(jnp.int32, (BLOCK, 1), 0)
    locals_[0].wait()
    for s in range(slots):
        k_sel[0, s] = k_all[chosen[s]]
    locals_[1].wait()
    for s in range(slots):
        limit = jnp.where(count > s, len_ref[0] - (first + chosen[s]) * BLOCK, 0)
        block = v_all[chosen[s]]
        v_sel[0, s] = jnp.where(row < limit, block.astype(F32), 0.0).astype(BF16)

    pl.semaphore_wait(barrier, chips)

    def pair(i, ref):
        return pltpu.make_async_remote_copy(
            ref.at[0], ref.at[1], pair_send.at[i], pair_recv.at[i], sibling, MESH
        )

    shared = [pair(i, ref) for i, ref in enumerate((k_sel, v_sel, wg, wu, wd))]

    def gather(buf, send, recv):
        return lambda k: pltpu.make_async_remote_copy(
            buf.at[0], buf.at[k], send.at[k], recv.at[k], peer(k), MESH
        )

    def scatter(obuf, rbuf, send, recv):
        return lambda g, k: pltpu.make_async_remote_copy(
            obuf.at[k, g], rbuf.at[k, g], send.at[k, g], recv.at[k, g], peer(k, True), MESH
        )

    queries = gather(qbuf, q_send, q_recv)
    normals = gather(nbuf, n_send, n_recv)
    attended = scatter(obuf_a, rbuf_a, a_send, a_recv)
    hidden = scatter(obuf_f, rbuf_f, f_send, f_recv)

    def total(copy, keep, rbuf):
        parts = []
        for g in range(groups):
            part = keep[g]
            if chips <= 8:
                for k in range(1, chips):
                    copy(g, k).wait_recv()
                    part = part + rbuf[k, g].astype(F32)
            else:

                def add(k, part, g=g):
                    copy(g, k).wait_recv()
                    return part + rbuf[k, g].astype(F32)

                part = lax.fori_loop(1, chips, add, part)
            parts.append(part)
        return jnp.concatenate(parts, axis=1)

    def put(i, g, columns, left, right, keep, obuf):
        w = left.shape[-1]
        both = jnp.concatenate([x.reshape(chunk, tokens, w) for x in (left, right)], axis=1)
        obuf[pl.ds(i * chunk, chunk), g, :, columns] = both.astype(BF16)

        def own():
            keep[g, :, columns] = both[0]

        if isinstance(i, int):
            if i == 0:
                own()
        else:
            pl.when(i == 0)(own)

    def halves(block):
        w = block.shape[-1]
        block = block.astype(F32).reshape(chunk, 2, tokens, w)
        return [block[:, i].reshape(chunk * tokens, w).astype(BF16) for i in range(2)]

    peers(lambda k: queries(k).start())
    shared[0].start()
    shared[1].start()
    peers(lambda k: queries(k).wait_recv())
    shared[0].wait_recv()
    shared[1].wait_recv()
    for copy in locals_[2:]:
        copy.wait()
    for copy in shared[2:]:
        copy.start()

    half_scale = 0.5 / math.sqrt(HDIM)

    def head(query, columns):
        keys = k_sel[:, :, :, columns].reshape(CORES * slots * BLOCK, HDIM)
        values = v_sel[:, :, :, columns].reshape(CORES * slots * BLOCK, HDIM)
        scores = lax.dot_general(query, keys, (((1,), (1,)), ((), ())), preferred_element_type=F32)
        weights = silu_of_twice(scores * half_scale).astype(BF16)
        return jnp.dot(weights, values, preferred_element_type=F32)

    for g in range(groups):

        def attend(i, g=g):
            for j in range(span // HDIM):
                at = g * span + j * HDIM
                left, right = halves(qbuf[pl.ds(i * chunk, chunk), :, pl.ds(at, HDIM)])
                left, right = head(left, pl.ds(at, HDIM)), head(right, pl.ds(half + at, HDIM))
                put(i, g, pl.ds(j * HDIM, HDIM), left, right, keep_a, obuf_a)

        loop(0, chips // chunk, attend)
        peers(lambda k, g=g: attended(g, k).start())

    attention = total(attended, keep_a, rbuf_a)
    stream = q_packed + attention * rms_scale(attention)
    nbuf[0] = (stream * rms_scale(stream)).astype(BF16)
    peers(lambda k: normals(k).start())
    for copy in shared[2:]:
        copy.wait_recv()
    peers(lambda k: normals(k).wait_recv())

    def activate(i):
        left, right = halves(nbuf[pl.ds(i * chunk, chunk)])

        def project(w):
            top = jnp.dot(left, w[:half], preferred_element_type=F32)
            return top + jnp.dot(right, w[half:], preferred_element_type=F32)

        return [
            (silu_of_twice(0.5 * project(wg.at[c])) * project(wu.at[c])).astype(BF16) for c in range(CORES)
        ]

    def feed(i, g, activation):
        def down(columns):
            return sum(
                jnp.dot(activation[c], wd[c, :, columns], preferred_element_type=F32) for c in range(CORES)
            )

        left, right = down(pl.ds(g * span, span)), down(pl.ds(half + g * span, span))
        put(i, g, slice(None), left, right, keep_f, obuf_f)

    if chips == chunk:
        activation = activate(0)
        for g in range(groups):
            feed(0, g, activation)
            peers(lambda k, g=g: hidden(g, k).start())
    else:

        def feed_all(i):
            activation = activate(i)
            for g in range(groups):
                feed(i, g, activation)

        loop(0, chips // chunk, feed_all)
        for g in range(groups):
            peers(lambda k, g=g: hidden(g, k).start())

    out_ref[...] = unpack(stream + total(hidden, keep_f, rbuf_f)).astype(out_ref.dtype)

    for copy in shared:
        copy.wait_send()
    peers(lambda k: queries(k).wait_send())
    peers(lambda k: normals(k).wait_send())
    for g in range(groups):
        peers(lambda k, g=g: attended(g, k).wait_send())
        peers(lambda k, g=g: hidden(g, k).wait_send())


def on_device(hist, queries, keys_cache, values_cache, sel_blocks, hist_len, w_gate, w_up, w_down):
    chips = hist // CORES
    tokens, width = queries.shape
    blocks_dev = keys_cache.shape[0] // BLOCK
    slots = max(1, blocks_dev // 2)
    hidden = w_gate.shape[1]
    blocked = (blocks_dev, BLOCK, width)
    packed = (2 * tokens, width // 2)
    groups = COLUMN_GROUPS if (width // 2) % (COLUMN_GROUPS * HDIM) == 0 else 1
    pieces = (groups, 2 * tokens, width // 2 // groups)
    exchange = [
        pltpu.VMEM(pieces, F32),
        pltpu.VMEM((chips,) + pieces, BF16),
        pltpu.VMEM((chips,) + pieces, BF16),
    ]
    smem = pl.BlockSpec(memory_space=pltpu.SMEM)
    vmem = pl.BlockSpec(memory_space=pltpu.VMEM)
    anywhere = pl.BlockSpec(memory_space=pl.ANY)
    return pl.pallas_call(
        functools.partial(kernel, chips),
        out_shape=jax.ShapeDtypeStruct((tokens, width), BF16),
        in_specs=[smem, smem, vmem] + [anywhere] * 5,
        out_specs=vmem,
        scratch_shapes=[
            pltpu.VMEM((chips,) + packed, BF16),
            pltpu.VMEM((chips,) + packed, BF16),
            *exchange,
            *exchange,
            pltpu.VMEM(blocked, BF16),
            pltpu.VMEM(blocked, BF16),
            pltpu.VMEM((CORES, slots, BLOCK, width), BF16),
            pltpu.VMEM((CORES, slots, BLOCK, width), BF16),
            pltpu.VMEM((CORES, width, hidden), BF16),
            pltpu.VMEM((CORES, width, hidden), BF16),
            pltpu.VMEM((CORES, hidden, width), BF16),
            *[pltpu.SemaphoreType.DMA((5,))] * 3,
            *[pltpu.SemaphoreType.DMA((chips,))] * 4,
            *[pltpu.SemaphoreType.DMA((chips, groups))] * 4,
        ],
        compiler_params=pltpu.CompilerParams(
            collective_id=0, has_side_effects=True, vmem_limit_bytes=56 * 1024 * 1024
        ),
    )(
        sel_blocks, hist_len, queries, keys_cache.reshape(blocked), values_cache.reshape(blocked),
        w_gate, w_up, w_down,
    )


def solution(mesh):
    placed = (
        P(("groups", "hist"), None),
        P(("groups", "hist"), None),
        P(("groups", "hist"), None),
        P("groups"),
        P("groups"),
        P(None, "hist"),
        P(None, "hist"),
        P("hist", None),
    )
    return jax.shard_map(
        functools.partial(on_device, mesh.shape["hist"]),
        mesh=mesh,
        in_specs=placed,
        out_specs=P(("groups", "hist"), None),
        check_vma=False,
    )
```

time: 42 us -> 37.2 us (0.89)
  Pallas kernels: 39.8 us -> 34.9 us
    pallas_call x1, Pallas kernels: 39.8 us -> 34.9 us  [on_device(): pl.pallas_call(functools.partial(kernel, chips), out_shape=jax.ShapeDtype...]
where the time goes in v2:
time: 37.2 us; the launch traced here: 37 us
  Pallas kernels  34.9 us (94%)
  local copies, waits for them, and re-layouts  1.35 us (4%)
  between operations  0.66 us (2%)
    pallas_call x1, Pallas kernels, on_device(): pl.pallas_call(functools.partial(kernel, chips), out_shape=jax.ShapeDtype...  34.9 us
    unnamed x1, local copies, waits for them, and re-layouts  1.35 us

profile of v2, /device:TPU:0, one launch (start us, length us, event | category | flops | bytes accessed | tf_op | source)
XLA Modules:
  0.0 37.0 jit_solution(8315354688075511439)
XLA Ops:
  0.7 34.9 %shard_map.82 = bf16[8,1536]{1,0:T(8,128)(2,1)} custom-call(s32[32]{0:T(128)} %sel_ref.1, s32[1]{0:T(128)S(6)} %copy.10.len_ref, bf16[8,1536]{1,0:T(8,128)(2,1)} %q_ref.1, bf16[8,128,1536]{2,1,0:T(8,128)(2,1)} %bitcast.2, bf16[8,128,1536]{2,1,0:T(8,128)(2,1)} %bitcast.3, bf16[1536,384]{1,0:T(8,128)(2,1)} %wg_hbm.1, bf16[1536,384]{1,0:T(8,128)(2,1)} %wu_hbm.1, ...), custom_call_target="tpu_custom_call" | custom-call | tf_op jit(solution)/shard_map/pallas_call | solution.py:280
  35.6 1.3 %copy.11 = bf16[8,1536]{1,0:T(8,128)(2,1)} copy(bf16[8,1536]{1,0:T(8,128)(2,1)} %shard_map.82) | data formatting | bytes 49152

commit v3 on v2

--- a/solution.py
+++ b/solution.py
@@ -11,7 +11,7 @@
 HDIM = 128
 BLOCK = 128
 CORES = 2
-COLUMN_GROUPS = 3
+COLUMN_GROUPS = 2
 MESH = pl.DeviceIdType.MESH
 F32 = jnp.float32
 BF16 = jnp.bfloat16
@@ -248,7 +248,7 @@
         for g in range(groups):
             peers(lambda k, g=g: hidden(g, k).start())
 
-    out_ref[...] = unpack(stream + total(hidden, keep_f, rbuf_f)).astype(out_ref.dtype)
+    out_ref[...] = unpack(stream + total(hidden, keep_f, rbuf_f))
 
     for copy in shared:
         copy.wait_send()
@@ -279,7 +279,7 @@
     anywhere = pl.BlockSpec(memory_space=pl.ANY)
     return pl.pallas_call(
         functools.partial(kernel, chips),
-        out_shape=jax.ShapeDtypeStruct((tokens, width), BF16),
+        out_shape=jax.ShapeDtypeStruct((tokens, width), F32),
         in_specs=[smem, smem, vmem] + [anywhere] * 5,
         out_specs=vmem,
         scratch_shapes=[
@@ -304,7 +304,7 @@
     )(
         sel_blocks, hist_len, queries, keys_cache.reshape(blocked), values_cache.reshape(blocked),
         w_gate, w_up, w_down,
-    )
+    ).astype(BF16)
 
 
 def solution(mesh):

time: 37.2 us -> 36.8 us (0.989)
  other arithmetic: 0 us -> 1.41 us
  local copies, waits for them, and re-layouts: 1.35 us -> 0 us
  Pallas kernels: 34.9 us -> 34.5 us
    convert_element_type x0 -> x1, other arithmetic: none -> 1.41 us  [on_device(): return pl.pallas_call(functools.partial(kernel, chips), out_shape=jax.Sha...]
    unnamed x1 -> x0, local copies, waits for them, and re-layouts: 1.35 us -> none
    pallas_call x1, Pallas kernels: 34.9 us -> 34.5 us  [on_device(): pl.pallas_call(functools.partial(kernel, chips), out_shape=jax.ShapeDtype...]
where the time goes in v3:
time: 36.8 us; the launch traced here: 36.6 us
  Pallas kernels  34.5 us (94%)
  other arithmetic  1.41 us (4%)
  between operations  0.66 us (2%)
    pallas_call x1, Pallas kernels, on_device(): pl.pallas_call(functools.partial(kernel, chips), out_shape=jax.ShapeDtype...  34.5 us
    convert_element_type x1, other arithmetic, on_device(): return pl.pallas_call(functools.partial(kernel, chips), out_shape=jax.Sha...  1.41 us

profile of v3, /device:TPU:0, one launch (start us, length us, event | category | flops | bytes accessed | tf_op | source)
XLA Modules:
  0.0 36.6 jit_solution(14348160863376572300)
XLA Ops:
  0.7 34.5 %shard_map.82 = f32[8,1536]{1,0:T(8,128)} custom-call(s32[32]{0:T(128)} %sel_ref.1, s32[1]{0:T(128)S(6)} %copy.9.len_ref, bf16[8,1536]{1,0:T(8,128)(2,1)} %q_ref.1, bf16[8,128,1536]{2,1,0:T(8,128)(2,1)} %bitcast.2, bf16[8,128,1536]{2,1,0:T(8,128)(2,1)} %bitcast.3, bf16[1536,384]{1,0:T(8,128)(2,1)} %wg_hbm.1, bf16[1536,384]{1,0:T(8,128)(2,1)} %wu_hbm.1, ...), custom_call_target="tpu_custom_call" | custom-call | tf_op jit(solution)/shard_map/pallas_call | solution.py:280
  35.2 1.4 %convert_element_type.3 = bf16[8,1536]{1,0:T(8,128)(2,1)} convert(f32[8,1536]{1,0:T(8,128)} %shard_map.82) | non-fusion elementwise | flops 12288 | bytes 73728 | tf_op jit(solution)/shard_map/convert_element_type | solution.py:307
